TPU v7x, 128 devices: a whole 4x4x4 slice. The times are simulated.
128 devices in a mesh: ctx: 8 (over x_hi, y), head: 8 (over z, core), var: 2 (over x_lo).
Axes of the slice: x: 4 (x_hi: 2, x_lo: 2; x = x_hi * 2 + x_lo), y: 4, z: 4, core: 2. Of those that a mesh axis runs over, the one named last changes fastest.
Arguments:
- sequence: bfloat16 [4096, 1536], P('ctx', 'head'), may hold values from -8 to 8
- deletions: int32 [8, 2], P('var'), parts along dimension 0, may hold values from 0 to 4096, as said below
- conv_taps: float32 [3, 1536], P(None, 'head'), may hold values from -3 to 3
- conv_bias: float32 [1536], P('head'), may hold values from -3 to 3
- w_proj: bfloat16 [1536, 3584], P(None, 'head'), may hold values from -1 to 1
- w_out: bfloat16 [1536, 1536], P('head'), may hold values from -0.15625 to 0.15625
- w_pair: bfloat16 [1536, 256], P('head'), may hold values from -0.15625 to 0.15625
- dist_table: float32 [16, 128], replicated, may hold values from -3 to 3
Outputs:
- pair_map: bfloat16 [8, 1024, 1024, 128], P('var', 'ctx', 'head'), parts along dimension 0
There are 2 independent parts, one for each index of `var`. A program takes and returns all parts, laid end to end along the dimension named above; an argument that names none is the same for every part. Nothing has to cross between parts.
Inputs may be any that keep to these rules, and one draw needn't show every extreme that they name: `deletions`: each variant deletes 1 to 128 consecutive tokens, some variant deletes exactly 128, and some variant's deletion ends at the last token of the locus.
All inputs are finite; a program needn't handle non-finite values.
Results may differ from a plain program's by a relative error of at most 0.025.
Values may be sent and summed in bfloat16 or wider, within the bound.
A program may use at most 128 MiB of HBM per device.

v0:
```python
import math
import jax
import jax.numpy as jnp
from jax import lax
from jax.sharding import PartitionSpec as P

HD = 128
VD = 192
C = 128
NB = 16
POOL = 4


def extended(block, sides, width):
    for axis, dim in sides:
        count = lax.axis_size(axis)
        forward = [(i, i + 1) for i in range(count - 1)]
        backward = [(target, source) for source, target in forward]
        low = lax.ppermute(
            lax.slice_in_dim(block, block.shape[dim] - width, None, axis=dim), axis, forward
        )
        high = lax.ppermute(lax.slice_in_dim(block, 0, width, axis=dim), axis, backward)
        block = jnp.concatenate([low, block, high], axis=dim)
    return block


def attend_block(running, queries, key_rows, value_rows):
    row_max, row_sum, weighted = running
    scores = jnp.einsum(
        "vqhe,vkhe->vhqk", queries, key_rows, preferred_element_type=jnp.float32
    ) / math.sqrt(queries.shape[-1])
    new_max = jnp.maximum(row_max, scores.max(-1))
    shrink = jnp.exp(row_max - new_max)
    weights = jnp.exp(scores - new_max[..., None])
    row_sum = row_sum * shrink + weights.sum(-1)
    weighted = weighted * shrink[..., None] + jnp.einsum(
        "vhqk,vkhe->vhqe",
        weights.astype(jnp.bfloat16),
        value_rows,
        preferred_element_type=jnp.float32,
    )
    return (new_max, row_sum, weighted)


def attend_rows(running, queries, key_rows, value_rows):
    key_total = key_rows.shape[1]
    block_rows = 512
    block_count = key_total // block_rows

    def block_step(block_index, state_now):
        key_part = lax.dynamic_slice_in_dim(key_rows, block_index * block_rows, block_rows, 1)
        value_part = lax.dynamic_slice_in_dim(value_rows, block_index * block_rows, block_rows, 1)
        return attend_block(state_now, queries, key_part, value_part)

    return lax.fori_loop(0, block_count, block_step, running)


def local(sequence, deletions, conv_taps, conv_bias, w_proj, w_out, w_pair, dist_table):
    token_count, local_width = sequence.shape
    variants = deletions.shape[0]
    head_count = w_out.shape[0] // VD
    row_start = lax.axis_index("ctx") * token_count
    positions = row_start + jnp.arange(token_count, dtype=jnp.int32)
    kept = jnp.logical_or(
        positions[None, :] < deletions[:, 0:1], positions[None, :] >= deletions[:, 1:2]
    )
    masked = jnp.where(kept[:, :, None], sequence[None], jnp.zeros((), jnp.bfloat16))
    dilation = token_count // 2
    padded = extended(masked, (("ctx", 1),), dilation)
    spread = padded.astype(jnp.float32)
    middle = spread[:, dilation : dilation + token_count]
    convolved = (
        conv_taps[0] * spread[:, :token_count]
        + conv_taps[1] * middle
        + conv_taps[2] * spread[:, 2 * dilation : 2 * dilation + token_count]
        + conv_bias
    )
    trunk_out = (middle + jax.nn.gelu(convolved, approximate=True)).astype(jnp.bfloat16)
    projected = jnp.einsum(
        "vtd,df->vtf",
        lax.all_gather(trunk_out, "head", axis=2, tiled=True),
        w_proj,
        preferred_element_type=jnp.float32,
    ).astype(jnp.bfloat16)
    projected = projected.reshape(trunk_out.shape[0], token_count, head_count, 2 * HD + VD)
    queries = projected[:variants, :, :, :HD]
    key_rows = projected[:, :, :, HD : 2 * HD]
    value_rows = projected[:, :, :, 2 * HD :]
    running = attend_rows(
        (
            jnp.full((variants, head_count, token_count), -jnp.inf, jnp.float32),
            jnp.zeros((variants, head_count, token_count), jnp.float32),
            jnp.zeros((variants, head_count, token_count, VD), jnp.float32),
        ),
        queries,
        lax.all_gather(key_rows, "ctx", axis=1, tiled=True),
        lax.all_gather(value_rows, "ctx", axis=1, tiled=True),
    )
    row_max, row_sum, weighted = running
    head_out = (weighted / row_sum[..., None]).astype(jnp.bfloat16)
    flat_out = head_out.transpose(0, 2, 1, 3).reshape(variants * token_count, head_count * VD)
    mixed_back = lax.psum_scatter(
        lax.dot_general(
            w_out, flat_out, (((0,), (1,)), ((), ())), preferred_element_type=jnp.float32
        ).astype(jnp.bfloat16),
        "head",
        scatter_dimension=0,
        tiled=True,
    ).astype(jnp.float32)
    residual = trunk_out.astype(jnp.float32) + mixed_back.T.reshape(
        variants, token_count, local_width
    )
    pooled = (
        residual.reshape(variants, token_count // POOL, POOL, local_width)
        .mean(2)
        .astype(jnp.bfloat16)
    )
    partial_value = jnp.einsum("vpd,dc->vpc", pooled, w_pair, preferred_element_type=jnp.float32)
    pair_proj = lax.psum(partial_value.astype(jnp.bfloat16), "head").astype(jnp.float32)
    row_feats = pair_proj[:, :, :C]
    all_cols = lax.all_gather(
        pair_proj[:, :, C:].astype(jnp.bfloat16), "ctx", axis=1, tiled=True
    ).astype(jnp.float32)
    col_count = all_cols.shape[1] // lax.axis_size("head")
    col_start = lax.axis_index("head") * col_count
    col_feats = lax.dynamic_slice_in_dim(all_cols, col_start, col_count, 1)
    row_ids = lax.axis_index("ctx") * (token_count // POOL) + jnp.arange(
        token_count // POOL, dtype=jnp.int32
    )
    col_ids = col_start + jnp.arange(col_count, dtype=jnp.int32)
    distance = jnp.abs(row_ids[:, None] - col_ids[None, :])
    buckets = jnp.zeros(distance.shape, jnp.int32)
    for power_index in range(NB - 1):
        buckets = buckets + (distance >= 2**power_index).astype(jnp.int32)
    one_hot = (buckets[:, :, None] == jnp.arange(NB, dtype=jnp.int32)).astype(jnp.float32)
    rel_table = jnp.dot(one_hot, dist_table, precision=lax.Precision.HIGHEST)
    pair_map = row_feats[:, :, None, :] + col_feats[:, None, :, :] + rel_table[None]
    return pair_map.astype(jnp.bfloat16)


def solution(mesh):
    in_specs = (
        P("ctx", "head"),
        P("var", None),
        P(None, "head"),
        P("head"),
        P(None, "head"),
        P("head", None),
        P("head", None),
        P(),
    )
    out_specs = P("var", "ctx", "head", None)
    return jax.shard_map(local, mesh=mesh, in_specs=in_specs, out_specs=out_specs, check_vma=False)
```

profile of v0, /device:TPU:0, one launch (start us, length us, event | category | flops | bytes accessed | tf_op | source)
XLA Modules:
  0.0 486.1 jit_solution(6132765217847577570)
XLA Ops:
  6.5 0.8 slice_bitcast_fusion.1
  7.4 1.0 broadcast_select_fusion
  8.5 3.6 collective-permute-start
  12.1 1.3 collective-permute-start.1
  13.4 7.0 %collective-permute-done = bf16[4,256,192]{1,2,0:T(8,128)(2,1)S(1)} collective-permute-done((bf16[4,256,192]{1,2,0:T(8,128)(2,1)S(1)}, bf16[4,256,192]{1,2,0:T(8,128)(2,1)S(1)}, u32[]{:S(2)}, u32[]{:S(2)}) %collective-permute-start) | collective-permute-done | bytes 393248 | tf_op jit(solution)/shard_map/ppermute | solution.py:19
  20.4 4.1 collective-permute-done.1
  25.0 1.8 copy-done.2
  26.8 2.0 fusion.28
  28.8 45.7 %all-gather.5.cloned.1.call-done = bf16[4,512,1536]{1,2,0:T(8,128)(2,1)} async-done(((bf16[4,512,192]{1,2,0:T(8,128)(2,1)}), bf16[4,512,1536]{1,2,0:T(8,128)(2,1)}) %all-gather.5.cloned.1.call-update) | async-done | bytes 6291472 | tf_op jit(solution)/shard_map/all_gather | solution.py:81
  74.5 5.8 %convert_bitcast_fusion = bf16[4,512,1,448]{1,3,0,2:T(8,128)(2,1)S(1)} fusion(bf16[4,512,1536]{1,2,0:T(8,128)(2,1)} %all-gather.5.cloned.1.call-done, bf16[1536,448]{0,1:T(8,128)(2,1)S(1)} %copy-done), kind=kOutput, calls=%fused_computation.29 | convolution fusion | flops 2819489792 | bytes 9502720 | tf_op jit(solution)/shard_map/vtd,df->vtf/dot_general | solution.py:79
  80.3 1.2 copy-done.4
  81.5 0.9 fusion.54
  82.5 2.1 slice.78
  85.0 71.1 %all-gather.7.cloned.1.call-done = bf16[4,4096,1,128]{1,3,0,2:T(8,128)(2,1)} async-done(((bf16[4,512,1,128]{1,3,0,2:T(8,128)(2,1)}), bf16[4,4096,1,128]{1,3,0,2:T(8,128)(2,1)}) %all-gather.7.cloned.1.call-update) | async-done | bytes 4194320 | tf_op jit(solution)/shard_map/all_gather | solution.py:96
  156.1 93.5 %all-gather.9.cloned.1.call-done = bf16[4,4096,1,192]{1,3,0,2:T(8,128)(2,1)} async-done(((bf16[4,512,1,192]{1,3,0,2:T(8,128)(2,1)}), bf16[4,4096,1,192]{1,3,0,2:T(8,128)(2,1)}) %all-gather.9.cloned.1.call-update) | async-done | bytes 6291472 | tf_op jit(solution)/shard_map/all_gather | solution.py:97
  249.6 40.1 %while.18 = (s32[]{:T(128)}, f32[4,1,512]{2,0,1:T(4,128)S(1)}, f32[4,1,512]{2,0,1:T(4,128)S(1)}, f32[4,1,512,192]{2,3,0,1:T(8,128)S(1)}, bf16[4,4096,1,128]{1,3,...) while((s32[]{:T(128)}, f32[4,1,512]{2,0,1:T(4,128)S(1)}, ...), condition=%wide.region_3.4_spmd.clone, body=%wide.region_0.3_spmd.clone.sunk | while | flops 680669184 | bytes 17694904 | solution.py:55
  249.6 1.8 bitcast_reduce_fusion.3
  252.1 2.4 bitcast_add_fusion.5
  254.6 1.8 bitcast_reduce_fusion.3
  257.1 2.4 bitcast_add_fusion.5
  259.6 1.8 bitcast_reduce_fusion.3
  261.5 0.7 fusion.67
  262.2 2.4 bitcast_add_fusion.5
  264.6 1.8 bitcast_reduce_fusion.3
  267.2 2.4 bitcast_add_fusion.5
  269.7 1.8 bitcast_reduce_fusion.3
  272.2 2.4 bitcast_add_fusion.5
  274.7 1.8 bitcast_reduce_fusion.3
  277.2 2.4 bitcast_add_fusion.5
  279.7 1.8 bitcast_reduce_fusion.3
  282.2 2.4 bitcast_add_fusion.5
  284.7 1.8 bitcast_reduce_fusion.3
  287.3 2.4 bitcast_add_fusion.5
  291.0 4.5 fusion.19
  295.6 8.7 %copy.38 = bf16[1536,2048]{1,0:T(8,128)(2,1)} copy(bf16[1536,2048]{0,1:T(8,128)(2,1)} %fusion.19) | data formatting | bytes 12582912
  304.5 40.6 %reduce-scatter.4.cloned.1.call-done = bf16[192,2048]{1,0:T(8,128)(2,1)} async-done(((bf16[1536,2048]{1,0:T(8,128)(2,1)}), bf16[192,2048]{1,0:T(8,128)(2,1)}) %reduce-scatter.4.cloned.1.call-update) | async-done | bytes 786448
  345.1 1.4 copy.39
  346.5 1.5 reshape.213
  348.0 2.9 copy.32
  351.0 3.6 convert_add_fusion
  354.6 2.0 copy.33
  357.5 1.0 convolution_convert_fusion.1
  358.5 59.7 %all-reduce.2.cloned.1.call-done = bf16[4,128,256]{2,1,0:T(8,128)(2,1)} async-done(((bf16[4,128,256]{2,1,0:T(8,128)(2,1)}), bf16[4,128,256]{2,1,0:T(8,128)(2,1)}) %all-reduce.2.cloned.1.call-update) | async-done | bytes 262160 | tf_op jit(solution)/shard_map/psum | solution.py:119
  418.2 1.6 slice_convert_fusion
  420.1 8.9 %fusion.33 = f32[128,128,128]{2,1,0:T(8,128)} fusion(s32[128,128]{1,0:T(8,128)S(1)} %convert_add_fusion.1, f32[16,128]{1,0:T(8,128)S(1)} %copy-done.7), kind=kOutput, calls=%fused_computation.50 | convolution fusion | flops 402915328 | bytes 8462336 | tf_op jit(solution)/shard_map/dot_general | solution.py:136
  429.0 36.8 %all-gather.11.cloned.1.call-done = bf16[4,1024,128]{2,1,0:T(8,128)(2,1)} async-done(((bf16[4,128,128]{2,1,0:T(8,128)(2,1)}), bf16[4,1024,128]{2,1,0:T(8,128)(2,1)}) %all-gather.11.cloned.1.call-update) | async-done | bytes 1048592 | tf_op jit(solution)/shard_map/all_gather | solution.py:121
  465.9 0.9 dynamic-slice_convert_fusion
  466.8 12.4 %add_convert_fusion = bf16[4,128,128,128]{3,2,1,0:T(8,128)(2,1)} fusion(f32[128,128,128]{2,1,0:T(8,128)} %fusion.33, f32[4,128,128]{2,1,0:T(8,128)S(1)} %dynamic-slice_convert_fusion, f32[4,128,128]{2,1,0:T(8,128)S(1)} %get-tuple-element.206), kind=kLoop, calls=%fused_computation.24 | loop fusion | flops 25165824 | bytes 25690112 | tf_op jit(solution)/shard_map/convert_element_type | solution.py:138
  (77 shorter events, 8.9 us)
Async XLA Ops:
  6.5 68.0 %copy-start = (bf16[1536,448]{0,1:T(8,128)(2,1)S(1)}, bf16[1536,448]{0,1:T(8,128)(2,1)}, u32[]{:S(2)}) copy-start(bf16[1536,448]{0,1:T(8,128)(2,1)} %param.14) | copy-start | bytes 4128772
  6.5 6.9 %copy-start.9 = (f32[3,192]{1,0:T(4,128)S(1)}, f32[3,192]{1,0:T(4,128)}, u32[]{:S(2)}) copy-start(f32[3,192]{1,0:T(4,128)} %param.12) | copy-start | bytes 6916
  6.5 68.0 %all-gather.5.cloned.1.call-start = ((), (), s32[]{:S(2)}) async-start(), calls=%async_computation.1 | async-start | bytes 7077888 | tf_op jit(solution)/shard_map/all_gather | solution.py:81
  8.5 11.9 %collective-permute-start = (bf16[4,256,192]{1,2,0:T(8,128)(2,1)S(1)}, bf16[4,256,192]{1,2,0:T(8,128)(2,1)S(1)}, u32[]{:S(2)}, u32[]{:S(2)}) collective-permute-start(bf16[4,256,192]{1,2,0:T(8,128)(2,1)S(1)} %get-tuple-element.204), channel_id=1, source_target_pairs={{0,16},{16,32},{32,48},{48,64},{64,80},{80,96},{96,112},{1,17},{17... | collective-permute-start | bytes 1179656 | tf_op jit(solution)/shard_map/ppermute | solution.py:19
  12.1 12.5 %collective-permute-start.1 = (bf16[4,256,192]{1,2,0:T(8,128)(2,1)S(1)}, bf16[4,256,192]{1,2,0:T(8,128)(2,1)S(1)}, u32[]{:S(2)}, u32[]{:S(2)}) collective-permute-start(bf16[4,256,192]{1,2,0:T(8,128)(2,1)S(1)} %get-tuple-element.205), channel_id=1, source_target_pairs={{16,0},{32,16},{48,32},{64,48},{80,64},{96,80},{112,96},{17,1},{33... | collective-permute-start | bytes 1179656 | tf_op jit(solution)/shard_map/ppermute | solution.py:22
  13.4 13.4 %copy-start.8 = (f32[192]{0:T(256)S(1)}, f32[192]{0:T(256)}, u32[]{:S(2)}) copy-start(f32[192]{0:T(256)} %param.13) | copy-start | bytes 2308
  25.0 1.8 copy-start.2
  28.8 127.3 %all-gather.7.cloned.1.call-start = ((), (), s32[]{:S(2)}) async-start(), calls=%async_computation.2 | async-start | bytes 4718592 | tf_op jit(solution)/shard_map/all_gather | solution.py:96
  80.3 1.2 copy-start.4
  82.4 167.1 %all-gather.9.cloned.1.call-start = ((), (), s32[]{:S(2)}) async-start(), calls=%async_computation.3 | async-start | bytes 7077888 | tf_op jit(solution)/shard_map/all_gather | solution.py:97
  84.6 260.5 %reduce-scatter.4.cloned.1.call-start = ((), (), s32[]{:S(2)}) async-start(), calls=%async_computation.6 | async-start | bytes 7077888
  289.9 1.1 copy-start.5
  304.3 113.9 %all-reduce.2.cloned.1.call-start = ((), (), s32[]{:S(2)}) async-start(), calls=%async_computation.4 | async-start | bytes 524288 | tf_op jit(solution)/shard_map/psum | solution.py:119
  348.0 2.9 copy-start.3
  356.6 0.9 copy-start.6
  357.2 63.0 %copy-start.7 = (f32[16,128]{1,0:T(8,128)S(1)}, f32[16,128]{1,0:T(8,128)}, u32[]{:S(2)}) copy-start(f32[16,128]{1,0:T(8,128)} %param.17) | copy-start | bytes 24580
  358.5 107.4 %all-gather.11.cloned.1.call-start = ((), (), s32[]{:S(2)}) async-start(), calls=%async_computation.5 | async-start | bytes 1179648 | tf_op jit(solution)/shard_map/all_gather | solution.py:121
  466.8 12.4 %copy-start.1 = (bf16[1536,448]{0,1:T(8,128)(2,1)S(1)}, bf16[1536,448]{0,1:T(8,128)(2,1)}, u32[]{:S(2)}) copy-start(bf16[1536,448]{0,1:T(8,128)(2,1)} %param.14) | copy-start | bytes 4128772
Sparse Core Ops, SparseCore 0:
  28.9 45.5 all-gather.4
  82.6 73.4 all-gather.6
  158.3 91.2 all-gather.8
  304.4 40.6 reduce-scatter.3
  358.6 59.6 all-reduce.1
  420.7 45.1 all-gather.10
where the time goes:
time: 488 us; the launch traced here: 486 us
  waiting for transfers between devices  359 us (74%)
  matrix products  54 us (11%)
  other arithmetic  30.4 us (6%)
  local copies, waits for them, and re-layouts  23.6 us (5%)
  between operations  13.7 us (3%)
  starting transfers between devices  5.27 us (1%)
    all_gather x1, waiting for transfers between devices, local(): lax.all_gather(value_rows, 'ctx', axis=1, tiled=True)  93.5 us
    all_gather x1, waiting for transfers between devices, local(): lax.all_gather(key_rows, 'ctx', axis=1, tiled=True)  71.1 us
    psum x1, waiting for transfers between devices, local(): lax.psum(partial_value.astype(jnp.bfloat16), 'head').astype(jnp.float32)  59.7 us
    all_gather x1, waiting for transfers between devices, local(): lax.all_gather(trunk_out, 'head', axis=2, tiled=True)  45.7 us
    unnamed x7, waiting for transfers between devices  40.6 us
    all_gather x1, waiting for transfers between devices, local(): lax.all_gather(pair_proj[:, :, C:].astype(jnp.bfloat16), 'ctx', axis=1, t...  36.8 us
    dot_general x8, matrix products, attend_block(): jnp.einsum('vhqk,vkhe->vhqe', weights.astype(jnp.bfloat16), value_rows, p...  19.3 us
    dot_general x8, matrix products, attend_block(): jnp.einsum('vqhe,vkhe->vhqk', queries, key_rows, preferred_element_type=j...  14.5 us
  transfers between devices with their start and end apart: 8, of which 8 were waited for; matrix products, arithmetic and copies ran while one was open for 2% of the time, Pallas kernels for 0%

commit v1 on v0

--- a/solution.py
+++ b/solution.py
@@ -116,7 +116,9 @@
         .astype(jnp.bfloat16)
     )
     partial_value = jnp.einsum("vpd,dc->vpc", pooled, w_pair, preferred_element_type=jnp.float32)
-    pair_proj = lax.psum(partial_value.astype(jnp.bfloat16), "head").astype(jnp.float32)
+    pair_proj = jnp.sum(lax.all_gather(partial_value.astype(jnp.bfloat16), "head"), axis=0).astype(
+        jnp.float32
+    )
     row_feats = pair_proj[:, :, :C]
     all_cols = lax.all_gather(
         pair_proj[:, :, C:].astype(jnp.bfloat16), "ctx", axis=1, tiled=True

time: 488 us -> 455 us (0.932)
  waiting for transfers between devices: 359 us -> 325 us
    psum x1 -> x0, waiting for transfers between devices: 59.7 us -> none  [local(): lax.psum(partial_value.astype(jnp.bfloat16), 'head').astype(jnp.float32)]
    all_gather x0 -> x1, waiting for transfers between devices: none -> 25.1 us  [local(): lax.all_gather(partial_value.astype(jnp.bfloat16), 'head')]
  transfers between devices with their start and end apart: 8 -> 8, of which waited for: 8 -> 8; matrix products, arithmetic and copies ran while one was open for 2% -> 3% of each run, Pallas kernels for 0% -> 0%
where the time goes in v1:
time: 455 us; the launch traced here: 453 us
  waiting for transfers between devices  325 us (71%)
  matrix products  54 us (12%)
  other arithmetic  31.4 us (7%)
  local copies, waits for them, and re-layouts  23.6 us (5%)
  between operations  13.7 us (3%)
  starting transfers between devices  5.27 us (1%)
    all_gather x1, waiting for transfers between devices, local(): lax.all_gather(value_rows, 'ctx', axis=1, tiled=True)  93.5 us
    all_gather x1, waiting for transfers between devices, local(): lax.all_gather(key_rows, 'ctx', axis=1, tiled=True)  71.1 us
    all_gather x1, waiting for transfers between devices, local(): lax.all_gather(trunk_out, 'head', axis=2, tiled=True)  45.7 us
    unnamed x7, waiting for transfers between devices  40.6 us
    all_gather x1, waiting for transfers between devices, local(): lax.all_gather(pair_proj[:, :, C:].astype(jnp.bfloat16), 'ctx', axis=1, t...  37.6 us
    all_gather x1, waiting for transfers between devices, local(): lax.all_gather(partial_value.astype(jnp.bfloat16), 'head')  25.1 us
    dot_general x8, matrix products, attend_block(): jnp.einsum('vhqk,vkhe->vhqe', weights.astype(jnp.bfloat16), value_rows, p...  19.3 us
    dot_general x8, matrix products, attend_block(): jnp.einsum('vqhe,vkhe->vhqk', queries, key_rows, preferred_element_type=j...  14.5 us
  transfers between devices with their start and end apart: 8, of which 8 were waited for; matrix products, arithmetic and copies ran while one was open for 3% of the time, Pallas kernels for 0%

profile of v1, /device:TPU:0, one launch (start us, length us, event | category | flops | bytes accessed | tf_op | source)
XLA Modules:
  0.0 453.2 jit_solution(3893172955179409513)
XLA Ops:
  6.5 0.8 slice_bitcast_fusion.1
  7.4 1.0 broadcast_select_fusion
  8.5 3.6 collective-permute-start
  12.1 1.3 collective-permute-start.1
  13.4 7.0 %collective-permute-done = bf16[4,256,192]{1,2,0:T(8,128)(2,1)S(1)} collective-permute-done((bf16[4,256,192]{1,2,0:T(8,128)(2,1)S(1)}, bf16[4,256,192]{1,2,0:T(8,128)(2,1)S(1)}, u32[]{:S(2)}, u32[]{:S(2)}) %collective-permute-start) | collective-permute-done | bytes 393248 | tf_op jit(solution)/shard_map/ppermute | solution.py:19
  20.4 4.1 collective-permute-done.1
  25.0 1.8 copy-done.2
  26.8 2.0 fusion.28
  28.8 45.7 %all-gather.7.cloned.1.call-done = bf16[4,512,1536]{1,2,0:T(8,128)(2,1)} async-done(((bf16[4,512,192]{1,2,0:T(8,128)(2,1)}), bf16[4,512,1536]{1,2,0:T(8,128)(2,1)}) %all-gather.7.cloned.1.call-update) | async-done | bytes 6291472 | tf_op jit(solution)/shard_map/all_gather | solution.py:81
  74.5 5.8 %convert_bitcast_fusion = bf16[4,512,1,448]{1,3,0,2:T(8,128)(2,1)S(1)} fusion(bf16[4,512,1536]{1,2,0:T(8,128)(2,1)} %all-gather.7.cloned.1.call-done, bf16[1536,448]{0,1:T(8,128)(2,1)S(1)} %copy-done), kind=kOutput, calls=%fused_computation.29 | convolution fusion | flops 2819489792 | bytes 9502720 | tf_op jit(solution)/shard_map/vtd,df->vtf/dot_general | solution.py:79
  80.3 1.2 copy-done.4
  81.5 0.9 fusion.54
  82.5 2.1 slice.78
  85.0 71.1 %all-gather.9.cloned.1.call-done = bf16[4,4096,1,128]{1,3,0,2:T(8,128)(2,1)} async-done(((bf16[4,512,1,128]{1,3,0,2:T(8,128)(2,1)}), bf16[4,4096,1,128]{1,3,0,2:T(8,128)(2,1)}) %all-gather.9.cloned.1.call-update) | async-done | bytes 4194320 | tf_op jit(solution)/shard_map/all_gather | solution.py:96
  156.1 93.5 %all-gather.11.cloned.1.call-done = bf16[4,4096,1,192]{1,3,0,2:T(8,128)(2,1)} async-done(((bf16[4,512,1,192]{1,3,0,2:T(8,128)(2,1)}), bf16[4,4096,1,192]{1,3,0,2:T(8,128)(2,1)}) %all-gather.11.cloned.1.call-update) | async-done | bytes 6291472 | tf_op jit(solution)/shard_map/all_gather | solution.py:97
  249.6 40.1 %while.18 = (s32[]{:T(128)}, f32[4,1,512]{2,0,1:T(4,128)S(1)}, f32[4,1,512]{2,0,1:T(4,128)S(1)}, f32[4,1,512,192]{2,3,0,1:T(8,128)S(1)}, bf16[4,4096,1,128]{1,3,...) while((s32[]{:T(128)}, f32[4,1,512]{2,0,1:T(4,128)S(1)}, ...), condition=%wide.region_3.4_spmd.clone, body=%wide.region_0.3_spmd.clone.sunk | while | flops 680669184 | bytes 17694904 | solution.py:55
  249.6 1.8 bitcast_reduce_fusion.3
  252.1 2.4 bitcast_add_fusion.5
  254.6 1.8 bitcast_reduce_fusion.3
  257.1 2.4 bitcast_add_fusion.5
  259.6 1.8 bitcast_reduce_fusion.3
  261.5 0.7 fusion.67
  262.2 2.4 bitcast_add_fusion.5
  264.6 1.8 bitcast_reduce_fusion.3
  267.2 2.4 bitcast_add_fusion.5
  269.7 1.8 bitcast_reduce_fusion.3
  272.2 2.4 bitcast_add_fusion.5
  274.7 1.8 bitcast_reduce_fusion.3
  277.2 2.4 bitcast_add_fusion.5
  279.7 1.8 bitcast_reduce_fusion.3
  282.2 2.4 bitcast_add_fusion.5
  284.7 1.8 bitcast_reduce_fusion.3
  287.3 2.4 bitcast_add_fusion.5
  291.0 4.5 %fusion.19 = bf16[1536,2048]{0,1:T(8,128)(2,1)} fusion(bf16[2048,192]{0,1:T(8,128)(2,1)S(1)} %bitcast.95, bf16[192,1536]{1,0:T(8,128)(2,1)S(1)} %copy-done.5), kind=kOutput, calls=%fused_computation.26 | convolution fusion | flops 1211105280 | bytes 7667712 | tf_op jit(solution)/shard_map/dot_general | solution.py:103
  295.6 8.7 %copy.38 = bf16[1536,2048]{1,0:T(8,128)(2,1)} copy(bf16[1536,2048]{0,1:T(8,128)(2,1)} %fusion.19) | data formatting | bytes 12582912
  304.5 40.6 %reduce-scatter.4.cloned.1.call-done = bf16[192,2048]{1,0:T(8,128)(2,1)} async-done(((bf16[1536,2048]{1,0:T(8,128)(2,1)}), bf16[192,2048]{1,0:T(8,128)(2,1)}) %reduce-scatter.4.cloned.1.call-update) | async-done | bytes 786448
  345.1 1.4 copy.39
  346.5 1.5 reshape.213
  348.0 2.9 copy.32
  351.0 3.6 convert_add_fusion
  354.6 2.0 copy.33
  357.5 1.0 convolution_convert_fusion.1
  358.5 25.1 %all-gather.15.cloned.1.call-done = bf16[32,128,256]{2,1,0:T(8,128)(2,1)} async-done(((bf16[4,128,256]{2,1,0:T(8,128)(2,1)}), bf16[32,128,256]{2,1,0:T(8,128)(2,1)}) %all-gather.15.cloned.1.call-update) | async-done | bytes 2097168 | tf_op jit(solution)/shard_map/all_gather | solution.py:119
  383.6 1.9 reduce_sum.35
  386.4 8.9 %fusion.33 = f32[128,128,128]{2,1,0:T(8,128)} fusion(s32[128,128]{1,0:T(8,128)S(1)} %convert_add_fusion.1, f32[16,128]{1,0:T(8,128)S(1)} %copy-done.7), kind=kOutput, calls=%fused_computation.50 | convolution fusion | flops 402915328 | bytes 8462336 | tf_op jit(solution)/shard_map/dot_general | solution.py:138
  395.3 37.6 %all-gather.13.cloned.1.call-done = bf16[4,1024,128]{2,1,0:T(8,128)(2,1)} async-done(((bf16[4,128,128]{2,1,0:T(8,128)(2,1)}), bf16[4,1024,128]{2,1,0:T(8,128)(2,1)}) %all-gather.13.cloned.1.call-update) | async-done | bytes 1048592 | tf_op jit(solution)/shard_map/all_gather | solution.py:123
  433.0 0.9 dynamic-slice_convert_fusion
  433.9 12.4 %add_convert_fusion = bf16[4,128,128,128]{3,2,1,0:T(8,128)(2,1)} fusion(f32[128,128,128]{2,1,0:T(8,128)} %fusion.33, f32[4,128,128]{2,1,0:T(8,128)S(1)} %dynamic-slice_convert_fusion, f32[4,128,128]{2,1,0:T(8,128)S(1)} %get-tuple-element.206), kind=kLoop, calls=%fused_computation.24 | loop fusion | flops 25165824 | bytes 25690112 | tf_op jit(solution)/shard_map/convert_element_type | solution.py:140
  (78 shorter events, 9.6 us)
Async XLA Ops:
  6.5 68.0 %copy-start = (bf16[1536,448]{0,1:T(8,128)(2,1)S(1)}, bf16[1536,448]{0,1:T(8,128)(2,1)}, u32[]{:S(2)}) copy-start(bf16[1536,448]{0,1:T(8,128)(2,1)} %param.14) | copy-start | bytes 4128772
  6.5 6.9 %copy-start.9 = (f32[3,192]{1,0:T(4,128)S(1)}, f32[3,192]{1,0:T(4,128)}, u32[]{:S(2)}) copy-start(f32[3,192]{1,0:T(4,128)} %param.12) | copy-start | bytes 6916
  6.5 68.0 %all-gather.7.cloned.1.call-start = ((), (), s32[]{:S(2)}) async-start(), calls=%async_computation.1 | async-start | bytes 7077888 | tf_op jit(solution)/shard_map/all_gather | solution.py:81
  8.5 11.9 %collective-permute-start = (bf16[4,256,192]{1,2,0:T(8,128)(2,1)S(1)}, bf16[4,256,192]{1,2,0:T(8,128)(2,1)S(1)}, u32[]{:S(2)}, u32[]{:S(2)}) collective-permute-start(bf16[4,256,192]{1,2,0:T(8,128)(2,1)S(1)} %get-tuple-element.204), channel_id=1, source_target_pairs={{0,16},{16,32},{32,48},{48,64},{64,80},{80,96},{96,112},{1,17},{17... | collective-permute-start | bytes 1179656 | tf_op jit(solution)/shard_map/ppermute | solution.py:19
  12.1 12.5 %collective-permute-start.1 = (bf16[4,256,192]{1,2,0:T(8,128)(2,1)S(1)}, bf16[4,256,192]{1,2,0:T(8,128)(2,1)S(1)}, u32[]{:S(2)}, u32[]{:S(2)}) collective-permute-start(bf16[4,256,192]{1,2,0:T(8,128)(2,1)S(1)} %get-tuple-element.205), channel_id=1, source_target_pairs={{16,0},{32,16},{48,32},{64,48},{80,64},{96,80},{112,96},{17,1},{33... | collective-permute-start | bytes 1179656 | tf_op jit(solution)/shard_map/ppermute | solution.py:22
  13.4 13.4 %copy-start.8 = (f32[192]{0:T(256)S(1)}, f32[192]{0:T(256)}, u32[]{:S(2)}) copy-start(f32[192]{0:T(256)} %param.13) | copy-start | bytes 2308
  25.0 1.8 copy-start.2
  28.8 127.3 %all-gather.9.cloned.1.call-start = ((), (), s32[]{:S(2)}) async-start(), calls=%async_computation.2 | async-start | bytes 4718592 | tf_op jit(solution)/shard_map/all_gather | solution.py:96
  80.3 1.2 copy-start.4
  82.4 167.1 %all-gather.11.cloned.1.call-start = ((), (), s32[]{:S(2)}) async-start(), calls=%async_computation.3 | async-start | bytes 7077888 | tf_op jit(solution)/shard_map/all_gather | solution.py:97
  84.6 260.5 %reduce-scatter.4.cloned.1.call-start = ((), (), s32[]{:S(2)}) async-start(), calls=%async_computation.6 | async-start | bytes 7077888
  289.9 1.1 copy-start.5
  304.3 79.2 %all-gather.15.cloned.1.call-start = ((), (), s32[]{:S(2)}) async-start(), calls=%async_computation.5 | async-start | bytes 2359296 | tf_op jit(solution)/shard_map/all_gather | solution.py:119
  348.0 2.9 copy-start.3
  356.6 0.9 copy-start.6
  358.5 74.5 %all-gather.13.cloned.1.call-start = ((), (), s32[]{:S(2)}) async-start(), calls=%async_computation.4 | async-start | bytes 1179648 | tf_op jit(solution)/shard_map/all_gather | solution.py:123
  383.6 2.9 copy-start.7
  433.9 12.4 %copy-start.1 = (bf16[1536,448]{0,1:T(8,128)(2,1)S(1)}, bf16[1536,448]{0,1:T(8,128)(2,1)}, u32[]{:S(2)}) copy-start(bf16[1536,448]{0,1:T(8,128)(2,1)} %param.14) | copy-start | bytes 4128772
Sparse Core Ops, SparseCore 0:
  28.9 45.5 all-gather.6
  82.6 73.4 all-gather.8
  158.3 91.2 all-gather.10
  304.4 40.6 reduce-scatter.3
  358.6 24.9 all-gather.14
  386.3 46.5 all-gather.12
